TPU v7x, 128 devices: a whole 4x4x4 slice. The times are simulated.
128 devices in a mesh: chan: 64 (over z_hi, x, y, core), pix: 2 (over z_lo).
Axes of the slice: x: 4, y: 4, z: 4 (z_hi: 2, z_lo: 2; z = z_hi * 2 + z_lo), core: 2. Of those that a mesh axis runs over, the one named last changes fastest.
Arguments:
- pol_cube: bfloat16 [2, 2304, 8, 2048], P(None, 'chan', None, 'pix'), may hold values from -96 to 96
- phasor: bfloat16 [2, 2304, 512], P(None, 'chan'), may hold values from -1 to 1, as said below
- chan_weight: float32 [2304], P('chan'), may hold values from 0.3 to 9
- flags: int32 [2304, 8], P('chan'), may hold values 0 or 1
Outputs:
- depth_cube: bfloat16 [2, 1024, 8, 2, 512], P('pix', 'chan')
Inputs may be any that keep to these rules, and one draw needn't show every extreme that they name: phasor[0] and phasor[1] are the cosine and sine of one angle.
All inputs are finite; a program needn't handle non-finite values. No bound on the sum of `flags` on one device may be relied on, other than what follows from the above.
Results may differ from a plain program's by a relative error of at most 0.0049.
Values may be sent and summed in bfloat16 or wider, within the bound.
A program may use at most 192 MiB of HBM per device.

v0:
```python
import jax
import jax.numpy as jnp
from jax import lax
from jax.sharding import PartitionSpec as P


def phase_matrix(block):
    real_part = block[0]
    imag_part = block[1]
    return jnp.stack(
        [jnp.stack([real_part, imag_part], 1), jnp.stack([-imag_part, real_part], 1)], 0
    )


def body(pol_cube, phasor, chan_weight, flags):
    weights = chan_weight[:, None] * flags.astype(jnp.float32)
    total = lax.psum(jnp.sum(weights, axis=0), "chan")
    weighted = (pol_cube.astype(jnp.float32) * weights[None, :, :, None]).astype(jnp.bfloat16)
    matrix = phase_matrix(phasor)
    summed = lax.psum_scatter(
        jnp.einsum("scrx,scod->xrod", weighted, matrix, preferred_element_type=jnp.float32),
        "chan",
        scatter_dimension=0,
        tiled=True,
    )
    result = (summed / total[None, :, None, None]).astype(jnp.bfloat16)
    return result[None]


def solution(mesh):
    placed = (P(None, "chan", None, "pix"), P(None, "chan", None), P("chan"), P("chan", None))
    return jax.shard_map(
        body,
        mesh=mesh,
        in_specs=placed,
        out_specs=P("pix", "chan", None, None, None),
        check_vma=False,
    )
```

profile of v0, /device:TPU:1, one launch (start us, length us, event | category | flops | bytes accessed | tf_op | source)
XLA Modules:
  0.0 452.6 jit_solution(8186208366395804137)
XLA Ops:
  6.5 0.0 reduce-scatter.2.cloned.1.call-start
  6.5 0.8 fusion.6
  7.3 0.1 copy.14
  7.4 1.1 fusion.8
  8.6 1.5 multiply_convert_fusion
  10.1 13.3 %convolution_bitcast_fusion = f32[1024,8,2,512]{0,3,1,2:T(8,128)} fusion(bf16[2,36,8,1024]{3,2,1,0:T(8,128)(2,1)S(1)} %multiply_convert_fusion, bf16[1,36,2,512]{3,1,0,2:T(8,128)(2,1)S(1)} %get-tuple-element.12, bf16[1,36,2,512]{3,1,0,2:T(8,128)(2,1)S(1)} %get-tuple-element.11), kind=kOutput, calls=%fused_computation | convolution fusion | flops 1208254464 | bytes 34881536 | tf_op jit(solution)/shard_map/scrx,scod->xrod/dot_general | solution.py:21
  23.4 34.2 %copy.16 = f32[1024,8,2,512]{3,1,2,0:T(8,128)} copy(f32[1024,8,2,512]{0,3,1,2:T(8,128)} %convolution_bitcast_fusion) | data formatting | bytes 67108864 | tf_op jit(solution)/shard_map/scrx,scod->xrod/transpose | solution.py:21
  57.5 0.0 reduce-scatter.2.cloned.1.call-update
  57.6 165.0 %psum.7 = f32[8]{0:T(128)S(1)} all-reduce(f32[8]{0:T(128)S(1)} %get-tuple-element.5), channel_id=1, replica_groups=mesh['chan'=64,'pix'=2] {'chan'}, use_global_device_ids=true, to_apply=%region_2.0 | all-reduce | flops 8 | bytes 64 | tf_op jit(solution)/shard_map/psum | solution.py:17
  222.6 221.1 %reduce-scatter.2.cloned.1.call-done = f32[16,8,2,512]{3,1,2,0:T(8,128)} async-done(((f32[1024,8,2,512]{3,1,2,0:T(8,128)}), f32[16,8,2,512]{3,1,2,0:T(8,128)}) %reduce-scatter.2.cloned.1.call-update) | async-done | bytes 524304 | tf_op jit(solution)/shard_map/reduce_scatter | solution.py:20
  443.7 1.2 fusion.2
  444.9 0.9 copy.17
  (3 shorter events, 0.0 us)
Async XLA Ops:
  6.5 437.2 %reduce-scatter.2.cloned.1.call-start = ((), (), s32[]{:S(2)}) async-start(), calls=%async_computation.1 | async-start | bytes 34078720 | tf_op jit(solution)/shard_map/reduce_scatter | solution.py:20
Sparse Core Ops, SparseCore 0:
  57.7 385.9 reduce-scatter.1
where the time goes:
time: 458 us; the launch traced here: 453 us
  waiting for transfers between devices  221 us (48%)
  blocking collectives  165 us (36%)
  local copies, waits for them, and re-layouts  36.3 us (8%)
  between operations  13.4 us (3%)
  matrix products  13.3 us (3%)
    reduce_scatter x1, waiting for transfers between devices, body(): lax.psum_scatter(jnp.einsum('scrx,scod->xrod', weighted, matrix, preferre...  221 us
    psum x1, blocking collectives, body(): total = lax.psum(jnp.sum(weights, axis=0), 'chan')  165 us
    transpose x1, local copies, waits for them, and re-layouts, body(): jnp.einsum('scrx,scod->xrod', weighted, matrix, preferred_element_type=jn...  34.2 us
    dot_general x1, matrix products, body(): jnp.einsum('scrx,scod->xrod', weighted, matrix, preferred_element_type=jn...  13.3 us
  transfers between devices with their start and end apart: 1, of which 1 were waited for; matrix products, arithmetic and copies ran while one was open for 0% of the time, Pallas kernels for 0%

commit v1 on v0

v1 whole, which is shorter than its diff:
```python
import jax
import jax.numpy as jnp
from jax import lax
from jax.experimental import pallas as pl
from jax.experimental.pallas import tpu as pltpu
from jax.sharding import PartitionSpec as P

MESH = pl.DeviceIdType.MESH
F32 = jnp.float32
BF16 = jnp.bfloat16

X, Y = 4, 4
CH = 36
BODY = 32
TAIL = CH - BODY
ROWS1 = 2 * BODY + 16
ROWS2 = 2 * BODY


def tdot(a, b):
    return lax.dot_general(a, b, (((0,), (0,)), ((), ())), preferred_element_type=F32)


def kernel(
    pol, phasor, cw, flags_t, out,
    wb, stage, s1, s2, r1, r2, pa, pb, tw, part, d2d, zsend, zrecv, tots,
    bal_s, bal_r, pol_s, pol_r, ph_s, ph_r, tw_s, tw_r, d_s, d_r, z_s, z_r, t_s, t_r, loc,
):
    me = lax.axis_index("chan")
    pix = lax.axis_index("pix")
    core = lax.rem(me, 2)
    y = lax.rem(me // 2, Y)
    x = lax.rem(me // (2 * Y), X)
    zh = me // (2 * X * Y)

    def dev(zz, xx, yy, cc):
        return (((zz * X + xx) * Y + yy) * 2 + cc, pix)

    def plane(dx, dy):
        return dev(zh, lax.rem(x + dx, X), lax.rem(y + dy, Y), core)

    core_peer = dev(zh, x, y, 1 - core)
    z_peer = dev(1 - zh, x, y, core)
    offsets = [(dx, dy) for dx in range(X) for dy in range(Y) if dx or dy]

    barrier = pltpu.get_barrier_semaphore()
    for target in [plane(dx, dy) for dx, dy in offsets] + [core_peer, z_peer]:
        pl.semaphore_signal(barrier, inc=1, device_id=target, device_id_type=MESH)

    re = phasor[0].astype(F32)
    im = phasor[1].astype(F32)
    re_t, im_t = re[BODY:], im[BODY:]
    block = jnp.concatenate([re[:BODY], im[:BODY], re_t, -im_t, im_t, re_t], axis=0).astype(BF16)
    pa[0, 0] = block[:, :256]
    pb[0, 0] = block[:, 256:]

    w = cw[...] * flags_t[...].astype(F32)
    for c in range(CH):
        wb[c] = jnp.broadcast_to(w[:, c : c + 1], (8, 128))
    row_sum = jnp.sum(w, axis=1, keepdims=True)
    lane = lax.broadcasted_iota(jnp.int32, (8, 128), 1)
    sub = lax.broadcasted_iota(jnp.int32, (8, 128), 0)
    tw[0] = jnp.sum(jnp.where(lane // 16 == sub, row_sum, 0.0), axis=0, keepdims=True)

    pl.semaphore_wait(barrier, len(offsets) + 2)

    def rcopy(src, dst, ss, rs, target):
        return pltpu.make_async_remote_copy(
            src_ref=src, dst_ref=dst, send_sem=ss, recv_sem=rs,
            device_id=target, device_id_type=MESH,
        )

    ph = {}

    def phasor_send(half, buf, have, to):
        k = half * 16 + to[0] * 4 + to[1]
        hop = (to[0] - have[0], to[1] - have[1])
        c = rcopy(buf.at[have], buf.at[to], ph_s.at[k], ph_r.at[k], plane(*hop))
        c.start()
        ph[(half,) + to] = c

    near = [1, 3, 2]
    for d in near:
        phasor_send(0, pa, (0, 0), (d, 0))
        phasor_send(1, pb, (0, 0), (0, d))
    for d in near:
        phasor_send(0, pa, (0, 0), (0, d))
        phasor_send(1, pb, (0, 0), (d, 0))

    tw_copies = []
    for dx, dy in offsets:
        k = dx * 4 + dy
        c = rcopy(tw.at[0], tw.at[k], tw_s.at[k], tw_r.at[k], plane(dx, dy))
        c.start()
        tw_copies.append(c)

    lane_b = lax.broadcasted_iota(jnp.int32, (1, 128), 1)

    def relayout(first, dx):
        xx = lax.rem(x + dx, X)
        zz = 1 - zh if first else zh
        at = pl.multiple_of((zz * X + xx) * 128, 128)
        other = pl.multiple_of((zh * X + xx) * 128, 128)
        rows = ROWS1 if first else ROWS2
        dst = s1 if first else s2
        for s in range(2):
            v = pol[s, :BODY, :, pl.ds(at, 128)].astype(F32) * wb[:BODY]
            stage[pl.ds(s * 256, 256), :] = v.reshape(256, 128)
        if first:
            for h, at_h in enumerate((at, other)):
                for s in range(2):
                    v = pol[s, BODY:, :, pl.ds(at_h, 128)].astype(F32) * wb[BODY:]
                    stage[pl.ds(512 + h * 64 + s * 32, 32), :] = v.reshape(32, 128)
        for q in range(rows // 16):
            v = [stage[pl.ds(q * 128 + r, 16, stride=8), :] for r in range(8)]
            for k in range(3):
                m = 1 << k
                mask = jnp.broadcast_to((lane_b // (16 * m)) % 2 == 1, (16, 128))
                new = list(v)
                for a in range(8):
                    if a & m:
                        continue
                    b = a | m
                    new[a] = jnp.where(mask, pltpu.roll(v[b], 16 * m, 1), v[a])
                    new[b] = jnp.where(mask, v[b], pltpu.roll(v[a], 128 - 16 * m, 1))
                v = new
            for g in range(8):
                dst[dx, g // 2, pl.ds(q * 16, 16), pl.ds((g % 2) * 128, 128)] = v[g].astype(BF16)

    pol_copies = ([], [])

    def send_pol(first, dx):
        src, dst = (s1, r1) if first else (s2, r2)
        for dy in range(Y):
            if dx == 0 and dy == 0:
                c = pltpu.make_async_copy(src.at[0, y], dst.at[0], loc.at[0 if first else 1])
            else:
                k = (0 if first else 16) + dx * 4 + dy
                c = rcopy(
                    src.at[dx, lax.rem(y + dy, Y)], dst.at[dx * 4 + dy],
                    pol_s.at[k], pol_r.at[k], plane(dx, dy),
                )
            c.start()
            pol_copies[0 if first else 1].append(c)

    for dx in (1, 3, 0, 2):
        relayout(True, dx)
        send_pol(True, dx)

    for d in near:
        ph[(0, d, 0)].wait_recv()
        for e in near:
            phasor_send(0, pa, (d, 0), (d, e))
        ph[(1, 0, d)].wait_recv()
        for e in near:
            phasor_send(1, pb, (0, d), (e, d))

    for dx in (1, 3, 0, 2):
        relayout(False, dx)
        send_pol(False, dx)

    for c in tw_copies:
        c.wait_recv()
    total = jnp.sum(tw[...], axis=0)
    tots[0] = total
    ct = rcopy(tots.at[0], tots.at[1], t_s.at[0], t_r.at[0], core_peer)
    ct.start()

    for d in range(X):
        for e in range(Y):
            if d or e:
                for half in range(2):
                    if not (half == 0 and e == 0) and not (half == 1 and d == 0):
                        ph[(half, d, e)].wait_recv()
    for c in pol_copies[0]:
        if c is pol_copies[0][8]:
            c.wait()
        else:
            c.wait_recv()

    row16 = lax.broadcasted_iota(jnp.int32, (256, 256), 0) % 16

    def contract(first, n):
        src = r1 if first else r2
        k, half = n // 2, n % 2
        p = (pa, pb)[half]
        w0 = src[:, :BODY].reshape(16 * BODY, 256)
        w1 = src[:, BODY : 2 * BODY].reshape(16 * BODY, 256)
        pr = p[:, :, :BODY].reshape(16 * BODY, 256)
        pi = p[:, :, BODY : 2 * BODY].reshape(16 * BODY, 256)
        lt = r1[:, 2 * BODY :].reshape(256, 256).astype(F32)
        pt = p[:, :, 2 * BODY :].reshape(256, 256)
        lt = jnp.where((row16 < 8) == first, lt, 0.0).astype(BF16)
        if first == (k == 1):
            shifted = pt.astype(F32)
            cut = 8 if first else 248
            pt = jnp.concatenate([shifted[cut:], shifted[:cut]], axis=0).astype(BF16)
        if k == 0:
            o = tdot(w0, pr) - tdot(w1, pi)
        else:
            o = tdot(w0, pi) + tdot(w1, pr)
        return o + tdot(lt, pt)

    mine = pl.multiple_of(core * 128, 128)
    theirs = pl.multiple_of((1 - core) * 128, 128)

    def spread(first, n):
        k = (0 if first else 4) + n
        part[k] = contract(first, n)
        c = rcopy(part.at[k, pl.ds(theirs, 128)], d2d.at[k], d_s.at[k], d_r.at[k], core_peer)
        c.start()
        return c

    d_copies = [spread(True, n) for n in range(4)]

    ct.wait_recv()
    plane_total = tots[0] + tots[1]
    tots[2] = plane_total
    cz = rcopy(tots.at[2], tots.at[3], t_s.at[1], t_r.at[1], z_peer)
    cz.start()

    z_copies = []
    for n in range(4):
        d_copies[n].wait_recv()
        zsend[n] = (part[n, pl.ds(mine, 128)] + d2d[n]).astype(BF16)
        c = rcopy(zsend.at[n], zrecv.at[n], z_s.at[n], z_r.at[n], z_peer)
        c.start()
        z_copies.append(c)

    for c in pol_copies[1]:
        if c is pol_copies[1][8]:
            c.wait()
        else:
            c.wait_recv()
    d_copies += [spread(False, n) for n in range(4)]

    cz.wait_recv()
    total = tots[2] + tots[3]
    ri = lax.broadcasted_iota(jnp.int32, (128, 128), 0)
    ci = lax.broadcasted_iota(jnp.int32, (128, 128), 1)
    column = jnp.sum(jnp.where(ri == ci, total, 0.0), axis=1, keepdims=True)
    for n in range(4):
        d_copies[4 + n].wait_recv()
        z_copies[n].wait_recv()
        summed = part[4 + n, pl.ds(mine, 128)] + d2d[4 + n] + zrecv[n].astype(F32)
        out[:, pl.ds(n * 256, 256)] = (summed / column).astype(BF16)

    for c in list(ph.values()) + tw_copies + [ct, cz] + d_copies + z_copies:
        c.wait_send()
    for group in pol_copies:
        for i, c in enumerate(group):
            if i != 8:
                c.wait_send()


def body(pol_cube, phasor, chan_weight, flags):
    vmem = pl.BlockSpec(memory_space=pltpu.VMEM)
    dma = pltpu.SemaphoreType.DMA
    out = pl.pallas_call(
        kernel,
        out_shape=jax.ShapeDtypeStruct((128, 1024), BF16),
        in_specs=[vmem] * 4,
        out_specs=vmem,
        scratch_shapes=[
            pltpu.VMEM((CH, 8, 128), F32),
            pltpu.VMEM((ROWS1 * 8, 128), F32),
            pltpu.VMEM((X, Y, ROWS1, 256), BF16),
            pltpu.VMEM((X, Y, ROWS2, 256), BF16),
            pltpu.VMEM((16, ROWS1, 256), BF16),
            pltpu.VMEM((16, ROWS2, 256), BF16),
            pltpu.VMEM((X, Y, ROWS1, 256), BF16),
            pltpu.VMEM((X, Y, ROWS1, 256), BF16),
            pltpu.VMEM((16, 1, 128), F32),
            pltpu.VMEM((8, 256, 256), F32),
            pltpu.VMEM((8, 128, 256), F32),
            pltpu.VMEM((4, 128, 256), BF16),
            pltpu.VMEM((4, 128, 256), BF16),
            pltpu.VMEM((4, 1, 128), F32),
            dma((1,)), dma((1,)),
            dma((32,)), dma((32,)),
            dma((32,)), dma((32,)),
            dma((16,)), dma((16,)),
            dma((8,)), dma((8,)),
            dma((4,)), dma((4,)),
            dma((2,)), dma((2,)),
            dma((2,)),
        ],
        compiler_params=pltpu.CompilerParams(
            collective_id=0, has_side_effects=True, vmem_limit_bytes=40 * 2**20
        ),
        cost_estimate=pl.CostEstimate(
            flops=2 * 512 * 1152 * 1024, bytes_accessed=2**21, transcendentals=0
        ),
        name="exchange",
    )(pol_cube, phasor, chan_weight[None, :], flags.T)
    return out.reshape(8, 16, 2, 512).transpose(1, 0, 2, 3)[None]


def solution(mesh):
    placed = (P(None, "chan", None, "pix"), P(None, "chan", None), P("chan"), P("chan", None))
    return jax.shard_map(
        body,
        mesh=mesh,
        in_specs=placed,
        out_specs=P("pix", "chan", None, None, None),
        check_vma=False,
    )
```

time: 458 us -> 45.6 us (0.10); the launches traced: 453 us -> 45.3 us
  waiting for transfers between devices: 221 us -> 0 us
  blocking collectives: 165 us -> 0 us
  Pallas kernels: 0 us -> 40.7 us
  local copies, waits for them, and re-layouts: 36.3 us -> 4.64 us
  between operations: 13.4 us -> 0.03 us
  matrix products: 13.3 us -> 0 us
    reduce_scatter x1 -> x0, waiting for transfers between devices: 221 us -> none  [body(): lax.psum_scatter(jnp.einsum('scrx,scod->xrod', weighted, matrix, preferre...]
    psum x1 -> x0, blocking collectives: 165 us -> none  [body(): total = lax.psum(jnp.sum(weights, axis=0), 'chan')]
    pallas_call x0 -> x1, Pallas kernels: none -> 40.7 us  [body(): pl.pallas_call(kernel, out_shape=jax.ShapeDtypeStruct((128, 1024), BF16),...]
    transpose x1 -> x0, local copies, waits for them, and re-layouts: 34.2 us -> none  [body(): jnp.einsum('scrx,scod->xrod', weighted, matrix, preferred_element_type=jn...]
    dot_general x1 -> x0, matrix products: 13.3 us -> none  [body(): jnp.einsum('scrx,scod->xrod', weighted, matrix, preferred_element_type=jn...]
  transfers between devices with their start and end apart: 1 -> 0, of which waited for: 1 -> 0; matrix products, arithmetic and copies ran while one was open for 0% -> 0% of each run, Pallas kernels for 0% -> 0%
where the time goes in v1:
time: 45.6 us; the launch traced here: 45.3 us
  Pallas kernels  40.7 us (89%)
  local copies, waits for them, and re-layouts  4.64 us (10%)
    pallas_call x1, Pallas kernels, body(): pl.pallas_call(kernel, out_shape=jax.ShapeDtypeStruct((128, 1024), BF16),...  40.7 us
    unnamed x7, local copies, waits for them, and re-layouts  3.5 us
    reshape x2, local copies, waits for them, and re-layouts, body(): return out.reshape(8, 16, 2, 512).transpose(1, 0, 2, 3)[None]  1.14 us

profile of v1, /device:TPU:1, one launch (start us, length us, event | category | flops | bytes accessed | tf_op | source)
XLA Modules:
  0.0 45.3 jit_solution(533670999702023367)
XLA Ops:
  0.0 0.9 %copy.5.phasor = bf16[2,36,512]{2,1,0:T(8,128)(2,1)S(1)} copy(bf16[2,36,512]{2,0,1:T(2,128)(2,1)} %param.5) | data formatting | bytes 147456 | tf_op args[1]
  0.9 0.0 copy-start
  0.9 1.3 %copy-done = bf16[2,36,8,1024]{3,2,1,0:T(8,128)(2,1)S(1)} copy-done((bf16[2,36,8,1024]{3,2,1,0:T(8,128)(2,1)S(1)}, bf16[2,36,8,1024]{3,2,1,0:T(8,128)(2,1)}, u32[]{:S(2)}) %copy-start) | copy-done | bytes 1179672
  2.2 0.0 copy-start.1
  2.2 0.7 %copy-done.1 = s32[36,8]{0,1:T(8,128)S(1)} copy-done((s32[36,8]{0,1:T(8,128)S(1)}, s32[36,8]{0,1:T(8,128)}, u32[]{:S(2)}) %copy-start.1) | copy-done | bytes 1176
  2.9 0.0 copy-start.2
  2.9 0.7 %copy-done.2 = f32[36]{0:T(128)S(1)} copy-done((f32[36]{0:T(128)S(1)}, f32[36]{0:T(128)}, u32[]{:S(2)}) %copy-start.2) | copy-done | bytes 168
  3.5 40.7 %exchange.1 = bf16[128,1024]{1,0:T(8,128)(2,1)S(1)} custom-call(bf16[2,36,8,1024]{3,2,1,0:T(8,128)(2,1)S(1)} %copy-done, bf16[2,36,512]{2,1,0:T(8,128)(2,1)S(1)} %copy.5.phasor, f32[1,36]{1,0:T(1,128)S(1)} %bitcast.8, s32[8,36]{1,0:T(8,128)S(1)} %bitcast.7), custom_call_target="tpu_custom_call" | custom-call | flops 1207959552 | bytes 2097152 | tf_op jit(solution)/shard_map/exchange/pallas_call | solution.py:259
  44.2 0.2 reshape.3
  44.4 1.0 %copy.8 = bf16[8,16,2,512]{3,2,0,1:T(2,128)(2,1)} copy(bf16[8,16,2,512]{3,2,1,0:T(2,128)(2,1)S(1)} %reshape.3) | data formatting | bytes 524288 | tf_op jit(solution)/shard_map/reshape | solution.py:296
Async XLA Ops:
  0.9 1.3 %copy-start = (bf16[2,36,8,1024]{3,2,1,0:T(8,128)(2,1)S(1)}, bf16[2,36,8,1024]{3,2,1,0:T(8,128)(2,1)}, u32[]{:S(2)}) copy-start(bf16[2,36,8,1024]{3,2,1,0:T(8,128)(2,1)} %pol.1) | copy-start | bytes 3538948
  2.2 0.7 %copy-start.1 = (s32[36,8]{0,1:T(8,128)S(1)}, s32[36,8]{0,1:T(8,128)}, u32[]{:S(2)}) copy-start(s32[36,8]{0,1:T(8,128)} %param.7) | copy-start | bytes 3460
  2.9 0.7 %copy-start.2 = (f32[36]{0:T(128)S(1)}, f32[36]{0:T(128)}, u32[]{:S(2)}) copy-start(f32[36]{0:T(128)} %param.6) | copy-start | bytes 436

commit v2 on v0

v2 whole, which is shorter than its diff:
```python
import jax
import jax.numpy as jnp
from jax import lax
from jax.experimental import pallas as pl
from jax.experimental.pallas import tpu as pltpu
from jax.sharding import PartitionSpec as P

MESH = pl.DeviceIdType.MESH
F32 = jnp.float32
BF16 = jnp.bfloat16

X, Y = 4, 4
CH = 36
BODY = 32
ROWS1 = 2 * BODY + 16
ROWS2 = 2 * BODY
PH_ROWS = ROWS1 + ROWS2


def tdot(a, b):
    return lax.dot_general(a, b, (((0,), (0,)), ((), ())), preferred_element_type=F32)


def kernel(
    pol_hbm, phasor_hbm, cw_hbm, flags_hbm, out,
    pol, phasor, cw, flags_t, wb, s1, s2, r1, r2, ph, tw, part, d2d, zsend, zrecv, tots,
    in_sem, pol_s, pol_r, ph_s, ph_r, tw_s, tw_r, d_s, d_r, z_s, z_r, t_s, t_r,
):
    me = lax.axis_index("chan")
    pix = lax.axis_index("pix")
    core = lax.rem(me, 2)
    y = lax.rem(me // 2, Y)
    x = lax.rem(me // (2 * Y), X)
    zh = me // (2 * X * Y)

    def dev(zz, xx, yy, cc):
        return (((zz * X + xx) * Y + yy) * 2 + cc, pix)

    def plane(dx, dy):
        return dev(zh, lax.rem(x + dx, X), lax.rem(y + dy, Y), core)

    core_peer = dev(zh, x, y, 1 - core)
    z_peer = dev(1 - zh, x, y, core)
    offsets = [(dx, dy) for dx in range(X) for dy in range(Y) if dx or dy]

    barrier = pltpu.get_barrier_semaphore()
    peers = [plane(dx, dy) for dx, dy in offsets] + [core_peer, z_peer]
    for target in peers:
        pl.semaphore_signal(barrier, inc=1, device_id=target, device_id_type=MESH)

    loads = [
        pltpu.make_async_copy(a, b, in_sem.at[i])
        for i, (a, b) in enumerate(
            ((flags_hbm, flags_t), (cw_hbm, cw), (phasor_hbm, phasor), (pol_hbm, pol))
        )
    ]
    for c in loads:
        c.start()

    i = lax.broadcasted_iota(jnp.int32, (256, 256), 0)
    j = lax.broadcasted_iota(jnp.int32, (256, 256), 1)
    order = jnp.where((i % 32) * 8 + i // 32 == j, 1.0, 0.0).astype(BF16)
    i, j = i[:128, :128], j[:128, :128]
    order_t = jnp.where((i % 16) * 8 + i // 16 == j, 1.0, 0.0).astype(BF16)

    loads[0].wait()
    loads[1].wait()
    w = cw[...] * flags_t[...].astype(F32)
    for c in range(CH):
        wb[c] = jnp.broadcast_to(w[:, c : c + 1], (8, 128))
    row_sum = jnp.sum(w, axis=1, keepdims=True)
    lane = lax.broadcasted_iota(jnp.int32, (8, 128), 1)
    sub = lax.broadcasted_iota(jnp.int32, (8, 128), 0)
    tw[0] = jnp.sum(jnp.where(lane // 16 == sub, row_sum, 0.0), axis=0, keepdims=True)

    loads[2].wait()
    both = phasor[...].astype(F32)
    re, im = both[:, 0], both[:, 1]
    tails = [jnp.concatenate([re[BODY:, h : h + 256], -im[BODY:, h : h + 256]], axis=0) for h in (0, 256)]
    block = jnp.concatenate(
        [re[:BODY, :256], im[:BODY, :256]] + tails + [re[:BODY, 256:], im[:BODY, 256:]], axis=0
    ).astype(BF16)
    ph[0, 0, 0] = block[:, :128]
    ph[1, 0, 0] = block[:, 128:]

    lane_b = lax.broadcasted_iota(jnp.int32, (1, 128), 1)

    def swap_blocks(v):
        for k in range(3):
            m = 1 << k
            mask = jnp.broadcast_to((lane_b // (16 * m)) % 2 == 1, v[0].shape)
            new = list(v)
            for a in range(8):
                if a & m:
                    continue
                b = a | m
                new[a] = jnp.where(mask, pltpu.roll(v[b], 16 * m, 1), v[a])
                new[b] = jnp.where(mask, v[b], pltpu.roll(v[a], 128 - 16 * m, 1))
            v = new
        return v

    def weighted(s, chans, at):
        v = pol[s, chans, :, pl.ds(at, 128)].astype(F32) * wb[chans]
        return v.reshape(-1, 128).astype(BF16)

    def regroup(matrix, v, rows):
        u = jnp.dot(matrix, v, preferred_element_type=F32).astype(BF16)
        return swap_blocks([u[r * rows : (r + 1) * rows] for r in range(8)])

    def relayout(first, dx):
        xx = lax.rem(x + dx, X)
        far = pl.multiple_of(((1 - zh) * X + xx) * 128, 128)
        near = pl.multiple_of((zh * X + xx) * 128, 128)
        dst = s1 if first else s2
        for s in range(2):
            v = regroup(order, weighted(s, slice(0, BODY), far if first else near), BODY)
            for g in range(8):
                dst[dx, g // 2, pl.ds(s * BODY, BODY), pl.ds((g % 2) * 128, 128)] = v[g]
        if first:
            v = [weighted(s, slice(BODY, CH), at) for at in (far, near) for s in range(2)]
            v = regroup(order_t, jnp.concatenate(v, axis=0), 16)
            for g in range(8):
                dst[dx, g // 2, pl.ds(2 * BODY, 16), pl.ds((g % 2) * 128, 128)] = v[g]

    loads[3].wait()
    near_x = (1, 3, 0, 2)
    for dx in near_x:
        relayout(True, dx)

    pl.semaphore_wait(barrier, len(peers))

    def rcopy(src, dst, ss, rs, target):
        return pltpu.make_async_remote_copy(
            src_ref=src, dst_ref=dst, send_sem=ss, recv_sem=rs,
            device_id=target, device_id_type=MESH,
        )

    def wait_for(view, sem):
        pltpu.make_async_copy(view, view, sem).wait()

    ring = (1, 3, 2)
    rest = pl.ds(1, 3)
    rows_a, rows_b = pl.ds(0, ROWS1), pl.ds(ROWS1, ROWS2)
    arrive = [
        ph.at[0, rest, 0],
        ph.at[1, 0, rest],
        ph.at[0, 0, rest],
        ph.at[1, rest, 0],
        ph.at[0, rest, rest, rows_a],
        ph.at[1, rest, rest, rows_a],
        ph.at[0, rest, rest, rows_b],
        ph.at[1, rest, rest, rows_b],
    ]
    for d in ring:
        rcopy(ph.at[0, 0, 0], ph.at[0, d, 0], ph_s.at[0], ph_r.at[0], plane(d, 0)).start()
        rcopy(ph.at[1, 0, 0], ph.at[1, 0, d], ph_s.at[1], ph_r.at[1], plane(0, d)).start()
    for d in ring:
        rcopy(ph.at[0, 0, 0], ph.at[0, 0, d], ph_s.at[2], ph_r.at[2], plane(0, d)).start()
        rcopy(ph.at[1, 0, 0], ph.at[1, d, 0], ph_s.at[3], ph_r.at[3], plane(d, 0)).start()

    def send_pol(first, dx):
        q = 0 if first else 1
        src, dst = (s1, r1) if first else (s2, r2)
        for dy in range(Y):
            if dx == 0 and dy == 0:
                pltpu.make_async_copy(src.at[0, y], dst.at[0], in_sem.at[4 + q]).start()
            else:
                rcopy(
                    src.at[dx, lax.rem(y + dy, Y)], dst.at[dx * 4 + dy],
                    pol_s.at[q], pol_r.at[q], plane(dx, dy),
                ).start()

    for dx, dy in offsets:
        k = dx * 4 + dy
        rcopy(tw.at[0], tw.at[k], tw_s.at[0], tw_r.at[0], plane(dx, dy)).start()

    for dx in near_x:
        send_pol(True, dx)

    def forward(q, strip, rows):
        for d in ring:
            if strip == 0:
                c = rcopy(
                    ph.at[0, rest, 0, rows], ph.at[0, rest, d, rows],
                    ph_s.at[q], ph_r.at[q], plane(0, d),
                )
            else:
                c = rcopy(
                    ph.at[1, 0, rest, rows], ph.at[1, d, rest, rows],
                    ph_s.at[q], ph_r.at[q], plane(d, 0),
                )
            c.start()

    wait_for(arrive[0], ph_r.at[0])
    forward(4, 0, rows_a)
    wait_for(arrive[1], ph_r.at[1])
    forward(5, 1, rows_a)
    forward(6, 0, rows_b)
    forward(7, 1, rows_b)

    for dx in near_x:
        relayout(False, dx)
        send_pol(False, dx)

    def contract(first, half):
        src = r1 if first else r2
        at = 0 if half == 0 else ROWS1
        w0 = src[:, :BODY].reshape(16 * BODY, 256)
        w1 = src[:, BODY : 2 * BODY].reshape(16 * BODY, 256)
        lt = r1[:, 2 * BODY :].astype(F32)
        lt = lt[:, :8] if first else lt[:, 8:]
        lt = lt.reshape(128, 256).astype(BF16)

        def lanes(lo, hi):
            return jnp.concatenate(
                [ph[s, :, :, lo:hi].reshape(-1, 128) for s in range(2)], axis=1
            )

        pr = lanes(at, at + BODY)
        pi = lanes(at + BODY, at + 2 * BODY)
        pt = lanes(2 * BODY, ROWS1).reshape(16, 16, 256).astype(F32)
        pt = pt[:, :8] if half == 0 else pt[:, 8:]
        turned = jnp.concatenate([-pt[:, 4:], pt[:, :4]], axis=1)
        pt = pt.reshape(128, 256).astype(BF16)
        turned = turned.reshape(128, 256).astype(BF16)
        yield tdot(w0, pr) - tdot(w1, pi) + tdot(lt, pt)
        yield tdot(w0, pi) + tdot(w1, pr) + tdot(lt, turned)

    mine = pl.multiple_of(core * 128, 128)
    theirs = pl.multiple_of((1 - core) * 128, 128)

    def spread(first, half):
        copies = []
        for k, value in enumerate(contract(first, half)):
            n = (0 if first else 4) + half * 2 + k
            part[n] = value
            c = rcopy(part.at[n, pl.ds(theirs, 128)], d2d.at[n], d_s.at[n], d_r.at[n], core_peer)
            c.start()
            copies.append(c)
        return copies

    d_copies, z_copies = [], []
    for g in (2, 3, 4, 5):
        wait_for(arrive[g], ph_r.at[g])
    wait_for(r1.at[pl.ds(1, 15)], pol_r.at[0])
    wait_for(r1.at[0], in_sem.at[4])
    for half in range(2):
        if half == 1:
            for g in (6, 7):
                wait_for(arrive[g], ph_r.at[g])
        d_copies += spread(True, half)
        for n in (half * 2, half * 2 + 1):
            d_copies[n].wait_recv()
            zsend[n] = (part[n, pl.ds(mine, 128)] + d2d[n]).astype(BF16)
            c = rcopy(zsend.at[n], zrecv.at[n], z_s.at[n], z_r.at[n], z_peer)
            c.start()
            z_copies.append(c)

    wait_for(tw.at[pl.ds(1, 15)], tw_r.at[0])
    tots[0] = jnp.sum(tw[...], axis=0)
    ct = rcopy(tots.at[0], tots.at[1], t_s.at[0], t_r.at[0], core_peer)
    ct.start()
    ct.wait_recv()
    tots[2] = tots[0] + tots[1]
    cz = rcopy(tots.at[2], tots.at[3], t_s.at[1], t_r.at[1], z_peer)
    cz.start()

    wait_for(r2.at[pl.ds(1, 15)], pol_r.at[1])
    wait_for(r2.at[0], in_sem.at[5])
    d_copies += spread(False, 0) + spread(False, 1)
    cz.wait_recv()
    total = tots[2] + tots[3]
    ri = lax.broadcasted_iota(jnp.int32, (128, 128), 0)
    ci = lax.broadcasted_iota(jnp.int32, (128, 128), 1)
    column = jnp.sum(jnp.where(ri == ci, total, 0.0), axis=1, keepdims=True)
    for n in range(4):
        z_copies[n].wait_recv()
        d_copies[4 + n].wait_recv()
        summed = part[4 + n, pl.ds(mine, 128)] + d2d[4 + n] + zrecv[n].astype(F32)
        out[:, pl.ds((n % 2) * 512 + (n // 2) * 256, 256)] = (summed / column).astype(BF16)

    for c in [ct, cz] + d_copies + z_copies:
        c.wait_send()
    for g in range(8):
        wait_for(arrive[g], ph_s.at[g])
    wait_for(r1.at[pl.ds(1, 15)], pol_s.at[0])
    wait_for(r2.at[pl.ds(1, 15)], pol_s.at[1])
    wait_for(tw.at[pl.ds(1, 15)], tw_s.at[0])


def body(pol_cube, phasor, chan_weight, flags):
    vmem = pltpu.VMEM
    dma = pltpu.SemaphoreType.DMA
    out = pl.pallas_call(
        kernel,
        out_shape=jax.ShapeDtypeStruct((128, 1024), BF16),
        in_specs=[pl.BlockSpec(memory_space=pltpu.HBM)] * 4,
        out_specs=pl.BlockSpec(memory_space=vmem),
        scratch_shapes=[
            vmem((2, CH, 8, 1024), BF16),
            vmem((CH, 2, 512), BF16),
            vmem((1, CH), F32),
            vmem((8, CH), jnp.int32),
            vmem((CH, 8, 128), F32),
            vmem((X, Y, ROWS1, 256), BF16),
            vmem((X, Y, ROWS2, 256), BF16),
            vmem((16, ROWS1, 256), BF16),
            vmem((16, ROWS2, 256), BF16),
            vmem((2, X, Y, PH_ROWS, 128), BF16),
            vmem((16, 1, 128), F32),
            vmem((8, 256, 256), F32),
            vmem((8, 128, 256), F32),
            vmem((4, 128, 256), BF16),
            vmem((4, 128, 256), BF16),
            vmem((4, 1, 128), F32),
            dma((6,)),
            dma((2,)), dma((2,)),
            dma((8,)), dma((8,)),
            dma((1,)), dma((1,)),
            dma((8,)), dma((8,)),
            dma((4,)), dma((4,)),
            dma((2,)), dma((2,)),
        ],
        compiler_params=pltpu.CompilerParams(
            collective_id=0, has_side_effects=True, vmem_limit_bytes=62 * 2**20
        ),
        cost_estimate=pl.CostEstimate(
            flops=2 * 512 * 1152 * 1024, bytes_accessed=2**21, transcendentals=0
        ),
        name="exchange",
    )(pol_cube, phasor.transpose(1, 0, 2), chan_weight[None, :], flags.T)
    return out.reshape(8, 16, 2, 512).transpose(1, 0, 2, 3)[None]


def solution(mesh):
    placed = (P(None, "chan", None, "pix"), P(None, "chan", None), P("chan"), P("chan", None))
    return jax.shard_map(
        body,
        mesh=mesh,
        in_specs=placed,
        out_specs=P("pix", "chan", None, None, None),
        check_vma=False,
    )
```

time: 458 us -> 38 us (0.08); the launches traced: 453 us -> 37.7 us
  waiting for transfers between devices: 221 us -> 0 us
  blocking collectives: 165 us -> 0 us
  Pallas kernels: 0 us -> 35.6 us
  local copies, waits for them, and re-layouts: 36.3 us -> 2.11 us
  between operations: 13.4 us -> 0.01 us
  matrix products: 13.3 us -> 0 us
    reduce_scatter x1 -> x0, waiting for transfers between devices: 221 us -> none  [body(): lax.psum_scatter(jnp.einsum('scrx,scod->xrod', weighted, matrix, preferre...]
    psum x1 -> x0, blocking collectives: 165 us -> none  [body(): total = lax.psum(jnp.sum(weights, axis=0), 'chan')]
    pallas_call x0 -> x1, Pallas kernels: none -> 35.6 us  [body(): pl.pallas_call(kernel, out_shape=jax.ShapeDtypeStruct((128, 1024), BF16),...]
    transpose x1 -> x0, local copies, waits for them, and re-layouts: 34.2 us -> none  [body(): jnp.einsum('scrx,scod->xrod', weighted, matrix, preferred_element_type=jn...]
    dot_general x1 -> x0, matrix products: 13.3 us -> none  [body(): jnp.einsum('scrx,scod->xrod', weighted, matrix, preferred_element_type=jn...]
  transfers between devices with their start and end apart: 1 -> 0, of which waited for: 1 -> 0; matrix products, arithmetic and copies ran while one was open for 0% -> 0% of each run, Pallas kernels for 0% -> 0%
where the time goes in v2:
time: 38 us; the launch traced here: 37.7 us
  Pallas kernels  35.6 us (94%)
  local copies, waits for them, and re-layouts  2.11 us (6%)
    pallas_call x1, Pallas kernels, body(): pl.pallas_call(kernel, out_shape=jax.ShapeDtypeStruct((128, 1024), BF16),...  35.6 us
    reshape x2, local copies, waits for them, and re-layouts, body(): return out.reshape(8, 16, 2, 512).transpose(1, 0, 2, 3)[None]  2.11 us

profile of v2, /device:TPU:1, one launch (start us, length us, event | category | flops | bytes accessed | tf_op | source)
XLA Modules:
  0.0 37.7 jit_solution(16122954189460932877)
XLA Ops:
  0.0 35.6 %exchange.1 = bf16[128,1024]{1,0:T(8,128)(2,1)} custom-call(bf16[2,36,8,1024]{3,2,1,0:T(8,128)(2,1)} %pol_hbm.1, bf16[36,2,512]{2,1,0:T(2,128)(2,1)} %bitcast.8, f32[1,36]{1,0:T(1,128)} %bitcast.10, s32[8,36]{1,0:T(8,128)} %bitcast.9), custom_call_target="tpu_custom_call" | custom-call | flops 1207959552 | bytes 2097152 | tf_op jit(solution)/shard_map/exchange/pallas_call | solution.py:294
  35.6 1.1 %reshape.3 = bf16[8,16,2,512]{3,2,1,0:T(2,128)(2,1)S(1)} reshape(bf16[128,1024]{1,0:T(8,128)(2,1)} %exchange.1) | data formatting | bytes 524288 | tf_op jit(solution)/shard_map/reshape | solution.py:332
  36.7 1.0 %copy.7 = bf16[8,16,2,512]{3,2,0,1:T(2,128)(2,1)} copy(bf16[8,16,2,512]{3,2,1,0:T(2,128)(2,1)S(1)} %reshape.3) | data formatting | bytes 524288 | tf_op jit(solution)/shard_map/reshape | solution.py:332

commit v3 on v2

--- a/solution.py
+++ b/solution.py
@@ -10,6 +10,7 @@
 BF16 = jnp.bfloat16
 
 X, Y = 4, 4
+SPREAD = [(dx, dy) for dx in (1, 3, 0, 2) for dy in range(Y) if dx or dy]
 CH = 36
 BODY = 32
 ROWS1 = 2 * BODY + 16
@@ -23,8 +24,8 @@
 
 def kernel(
     pol_hbm, phasor_hbm, cw_hbm, flags_hbm, out,
-    pol, phasor, cw, flags_t, wb, s1, s2, r1, r2, ph, tw, part, d2d, zsend, zrecv, tots,
-    in_sem, pol_s, pol_r, ph_s, ph_r, tw_s, tw_r, d_s, d_r, z_s, z_r, t_s, t_r,
+    pol, phasor, cw, flags_t, order_o, wb, s1, s2, r1, r2, ph, tw, part, d2d, zsend, zrecv, tots,
+    in_sem, pol_s, pol_r, ph_s, ph_r, tw_s, tw_r, d_s, d_r, z_s, z_r, t_s, t_r, ready,
 ):
     me = lax.axis_index("chan")
     pix = lax.axis_index("pix")
@@ -44,9 +45,13 @@
     offsets = [(dx, dy) for dx in range(X) for dy in range(Y) if dx or dy]
 
     barrier = pltpu.get_barrier_semaphore()
-    peers = [plane(dx, dy) for dx, dy in offsets] + [core_peer, z_peer]
+    peers = [plane(dx, dy) for dx, dy in offsets] + [core_peer]
     for target in peers:
         pl.semaphore_signal(barrier, inc=1, device_id=target, device_id_type=MESH)
+
+    @pl.when(zh == 0)
+    def _():
+        pl.semaphore_signal(barrier, inc=1, device_id=z_peer, device_id_type=MESH)
 
     loads = [
         pltpu.make_async_copy(a, b, in_sem.at[i])
@@ -62,6 +67,12 @@
     order = jnp.where((i % 32) * 8 + i // 32 == j, 1.0, 0.0).astype(BF16)
     i, j = i[:128, :128], j[:128, :128]
     order_t = jnp.where((i % 16) * 8 + i // 16 == j, 1.0, 0.0).astype(BF16)
+
+    i = lax.broadcasted_iota(jnp.int32, (256, 128), 0)
+    j = lax.broadcasted_iota(jnp.int32, (256, 128), 1)
+    at_row = (i // 2) % 8 * 16 + i // 16 == j
+    for k in range(2):
+        order_o[k] = jnp.where(at_row & (i % 2 == k), 1.0, 0.0).astype(BF16)
 
     loads[0].wait()
     loads[1].wait()
@@ -127,7 +138,11 @@
     for dx in near_x:
         relayout(True, dx)
 
-    pl.semaphore_wait(barrier, len(peers))
+    pl.semaphore_wait(barrier, len(peers) + zh)
+
+    @pl.when(zh == 1)
+    def _():
+        pl.semaphore_signal(ready, inc=1, device_id=z_peer, device_id_type=MESH)
 
     def rcopy(src, dst, ss, rs, target):
         return pltpu.make_async_remote_copy(
@@ -158,24 +173,21 @@
         rcopy(ph.at[0, 0, 0], ph.at[0, 0, d], ph_s.at[2], ph_r.at[2], plane(0, d)).start()
         rcopy(ph.at[1, 0, 0], ph.at[1, d, 0], ph_s.at[3], ph_r.at[3], plane(d, 0)).start()
 
-    def send_pol(first, dx):
+    def send_pol(first, dx, dy):
         q = 0 if first else 1
         src, dst = (s1, r1) if first else (s2, r2)
-        for dy in range(Y):
-            if dx == 0 and dy == 0:
-                pltpu.make_async_copy(src.at[0, y], dst.at[0], in_sem.at[4 + q]).start()
-            else:
-                rcopy(
-                    src.at[dx, lax.rem(y + dy, Y)], dst.at[dx * 4 + dy],
-                    pol_s.at[q], pol_r.at[q], plane(dx, dy),
-                ).start()
-
+        rcopy(
+            src.at[dx, lax.rem(y + dy, Y)], dst.at[dx * 4 + dy],
+            pol_s.at[q], pol_r.at[q], plane(dx, dy),
+        ).start()
+
+    pltpu.make_async_copy(s1.at[0, y], r1.at[0], in_sem.at[4]).start()
     for dx, dy in offsets:
         k = dx * 4 + dy
         rcopy(tw.at[0], tw.at[k], tw_s.at[0], tw_r.at[0], plane(dx, dy)).start()
 
-    for dx in near_x:
-        send_pol(True, dx)
+    for dx, dy in SPREAD:
+        send_pol(True, dx, dy)
 
     def forward(q, strip, rows):
         for d in ring:
@@ -200,7 +212,14 @@
 
     for dx in near_x:
         relayout(False, dx)
-        send_pol(False, dx)
+    pltpu.make_async_copy(s2.at[0, y], r2.at[0], in_sem.at[5]).start()
+    for dx, dy in SPREAD:
+        send_pol(False, dx, dy)
+
+    wait_for(tw.at[pl.ds(1, 15)], tw_r.at[0])
+    tots[0] = jnp.sum(tw[...], axis=0)
+    ct = rcopy(tots.at[0], tots.at[1], t_s.at[0], t_r.at[0], core_peer)
+    ct.start()
 
     def contract(first, half):
         src = r1 if first else r2
@@ -244,26 +263,26 @@
         wait_for(arrive[g], ph_r.at[g])
     wait_for(r1.at[pl.ds(1, 15)], pol_r.at[0])
     wait_for(r1.at[0], in_sem.at[4])
+    @pl.when(zh == 0)
+    def _():
+        pl.semaphore_wait(ready, 1)
+
     for half in range(2):
         if half == 1:
             for g in (6, 7):
                 wait_for(arrive[g], ph_r.at[g])
         d_copies += spread(True, half)
+        if half == 0:
+            ct.wait_recv()
+            tots[2] = tots[0] + tots[1]
+            cz = rcopy(tots.at[2], tots.at[3], t_s.at[1], t_r.at[1], z_peer)
+            cz.start()
         for n in (half * 2, half * 2 + 1):
             d_copies[n].wait_recv()
             zsend[n] = (part[n, pl.ds(mine, 128)] + d2d[n]).astype(BF16)
             c = rcopy(zsend.at[n], zrecv.at[n], z_s.at[n], z_r.at[n], z_peer)
             c.start()
             z_copies.append(c)
-
-    wait_for(tw.at[pl.ds(1, 15)], tw_r.at[0])
-    tots[0] = jnp.sum(tw[...], axis=0)
-    ct = rcopy(tots.at[0], tots.at[1], t_s.at[0], t_r.at[0], core_peer)
-    ct.start()
-    ct.wait_recv()
-    tots[2] = tots[0] + tots[1]
-    cz = rcopy(tots.at[2], tots.at[3], t_s.at[1], t_r.at[1], z_peer)
-    cz.start()
 
     wait_for(r2.at[pl.ds(1, 15)], pol_r.at[1])
     wait_for(r2.at[0], in_sem.at[5])
@@ -273,11 +292,16 @@
     ri = lax.broadcasted_iota(jnp.int32, (128, 128), 0)
     ci = lax.broadcasted_iota(jnp.int32, (128, 128), 1)
     column = jnp.sum(jnp.where(ri == ci, total, 0.0), axis=1, keepdims=True)
-    for n in range(4):
-        z_copies[n].wait_recv()
-        d_copies[4 + n].wait_recv()
-        summed = part[4 + n, pl.ds(mine, 128)] + d2d[4 + n] + zrecv[n].astype(F32)
-        out[:, pl.ds((n % 2) * 512 + (n // 2) * 256, 256)] = (summed / column).astype(BF16)
+    for half in range(2):
+        rows = 0.0
+        for k in range(2):
+            n = half * 2 + k
+            z_copies[n].wait_recv()
+            d_copies[4 + n].wait_recv()
+            summed = part[4 + n, pl.ds(mine, 128)] + d2d[4 + n] + zrecv[n].astype(F32)
+            value = (summed / column).astype(BF16)
+            rows = rows + jnp.dot(order_o[k], value, preferred_element_type=F32)
+        out[:, :, pl.ds(half * 256, 256)] = rows.astype(BF16).reshape(128, 2, 256)
 
     for c in [ct, cz] + d_copies + z_copies:
         c.wait_send()
@@ -293,7 +317,7 @@
     dma = pltpu.SemaphoreType.DMA
     out = pl.pallas_call(
         kernel,
-        out_shape=jax.ShapeDtypeStruct((128, 1024), BF16),
+        out_shape=jax.ShapeDtypeStruct((128, 2, 512), BF16),
         in_specs=[pl.BlockSpec(memory_space=pltpu.HBM)] * 4,
         out_specs=pl.BlockSpec(memory_space=vmem),
         scratch_shapes=[
@@ -301,6 +325,7 @@
             vmem((CH, 2, 512), BF16),
             vmem((1, CH), F32),
             vmem((8, CH), jnp.int32),
+            vmem((2, 256, 128), BF16),
             vmem((CH, 8, 128), F32),
             vmem((X, Y, ROWS1, 256), BF16),
             vmem((X, Y, ROWS2, 256), BF16),
@@ -320,16 +345,17 @@
             dma((8,)), dma((8,)),
             dma((4,)), dma((4,)),
             dma((2,)), dma((2,)),
+            pltpu.SemaphoreType.REGULAR,
         ],
         compiler_params=pltpu.CompilerParams(
-            collective_id=0, has_side_effects=True, vmem_limit_bytes=62 * 2**20
+            collective_id=0, has_side_effects=True, vmem_limit_bytes=40 * 2**20
         ),
         cost_estimate=pl.CostEstimate(
             flops=2 * 512 * 1152 * 1024, bytes_accessed=2**21, transcendentals=0
         ),
         name="exchange",
-    )(pol_cube, phasor.transpose(1, 0, 2), chan_weight[None, :], flags.T)
-    return out.reshape(8, 16, 2, 512).transpose(1, 0, 2, 3)[None]
+    )(*[pltpu.with_memory_space_constraint(a, pltpu.HBM) for a in (pol_cube, phasor.transpose(1, 0, 2), chan_weight[None, :], flags.T)])
+    return out.reshape(1, 16, 8, 2, 512)
 
 
 def solution(mesh):

time: 38 us -> 35.9 us (0.945)
  local copies, waits for them, and re-layouts: 2.11 us -> 0.71 us
  Pallas kernels: 35.6 us -> 35 us
    reshape x2 -> x0, local copies, waits for them, and re-layouts: 2.11 us -> none  [body(): return out.reshape(8, 16, 2, 512).transpose(1, 0, 2, 3)[None]]
    unnamed x0 -> x1, local copies, waits for them, and re-layouts: none -> 0.71 us
    pallas_call x1, Pallas kernels: 35.6 us -> 35 us  [body(): pl.pallas_call(kernel, out_shape=jax.ShapeDtypeStruct((128, 2, 512), BF16...]
where the time goes in v3:
time: 35.9 us; the launch traced here: 35.7 us
  Pallas kernels  35 us (97%)
  local copies, waits for them, and re-layouts  0.71 us (2%)
    pallas_call x1, Pallas kernels, body(): pl.pallas_call(kernel, out_shape=jax.ShapeDtypeStruct((128, 2, 512), BF16...  35 us

profile of v3, /device:TPU:1, one launch (start us, length us, event | category | flops | bytes accessed | tf_op | source)
XLA Modules:
  0.0 35.7 jit_solution(1507405495111931181)
XLA Ops:
  0.0 35.0 %exchange.1 = bf16[128,2,512]{2,1,0:T(2,128)(2,1)S(1)} custom-call(bf16[2,36,8,1024]{3,2,1,0:T(8,128)(2,1)} %pol_hbm.1, bf16[36,2,512]{2,1,0:T(2,128)(2,1)} %bitcast.5, f32[1,36]{1,0:T(1,128)} %bitcast.7, s32[8,36]{1,0:T(8,128)} %bitcast.6), custom_call_target="tpu_custom_call" | custom-call | flops 1207959552 | bytes 2097152 | tf_op jit(solution)/shard_map/exchange/pallas_call | solution.py:318
  35.0 0.7 %copy.6 = bf16[1,16,8,2,512]{4,3,2,1,0:T(2,128)(2,1)} copy(bf16[1,16,8,2,512]{4,3,2,1,0:T(2,128)(2,1)S(1)} %bitcast.4) | data formatting | bytes 524288

commit v4 on v3

--- a/solution.py
+++ b/solution.py
@@ -16,6 +16,7 @@
 ROWS1 = 2 * BODY + 16
 ROWS2 = 2 * BODY
 PH_ROWS = ROWS1 + ROWS2
+POL_ROWS = 4 * BODY + 16
 
 
 def tdot(a, b):
@@ -65,8 +66,8 @@
     i = lax.broadcasted_iota(jnp.int32, (256, 256), 0)
     j = lax.broadcasted_iota(jnp.int32, (256, 256), 1)
     order = jnp.where((i % 32) * 8 + i // 32 == j, 1.0, 0.0).astype(BF16)
-    i, j = i[:128, :128], j[:128, :128]
-    order_t = jnp.where((i % 16) * 8 + i // 16 == j, 1.0, 0.0).astype(BF16)
+    i, j = i[:64, :64], j[:64, :64]
+    order_t = jnp.where((i % 8) * 8 + i // 8 == j, 1.0, 0.0).astype(BF16)
 
     i = lax.broadcasted_iota(jnp.int32, (256, 128), 0)
     j = lax.broadcasted_iota(jnp.int32, (256, 128), 1)
@@ -114,24 +115,23 @@
         v = pol[s, chans, :, pl.ds(at, 128)].astype(F32) * wb[chans]
         return v.reshape(-1, 128).astype(BF16)
 
-    def regroup(matrix, v, rows):
-        u = jnp.dot(matrix, v, preferred_element_type=F32).astype(BF16)
+    def regroup(matrix, v, rows, kind):
+        u = jnp.dot(matrix, v, preferred_element_type=F32).astype(kind)
         return swap_blocks([u[r * rows : (r + 1) * rows] for r in range(8)])
 
     def relayout(first, dx):
         xx = lax.rem(x + dx, X)
-        far = pl.multiple_of(((1 - zh) * X + xx) * 128, 128)
-        near = pl.multiple_of((zh * X + xx) * 128, 128)
+        at = pl.multiple_of(((1 - zh if first else zh) * X + xx) * 128, 128)
         dst = s1 if first else s2
         for s in range(2):
-            v = regroup(order, weighted(s, slice(0, BODY), far if first else near), BODY)
+            v = regroup(order, weighted(s, slice(0, BODY), at), BODY, BF16)
             for g in range(8):
-                dst[dx, g // 2, pl.ds(s * BODY, BODY), pl.ds((g % 2) * 128, 128)] = v[g]
-        if first:
-            v = [weighted(s, slice(BODY, CH), at) for at in (far, near) for s in range(2)]
-            v = regroup(order_t, jnp.concatenate(v, axis=0), 16)
-            for g in range(8):
-                dst[dx, g // 2, pl.ds(2 * BODY, 16), pl.ds((g % 2) * 128, 128)] = v[g]
+                dst[dx, g // 2, pl.ds((g % 2) * 2 * BODY + s * BODY, BODY), :] = v[g]
+        v = [weighted(s, slice(BODY, CH), at) for s in range(2)]
+        v = regroup(order_t, jnp.concatenate(v, axis=0), 8, F32)
+        for yy in range(Y):
+            tail = jnp.concatenate([v[2 * yy], v[2 * yy + 1]], axis=0)
+            dst[dx, yy, pl.ds(4 * BODY, 16), :] = tail.astype(BF16)
 
     loads[3].wait()
     near_x = (1, 3, 0, 2)
@@ -213,8 +213,6 @@
     for dx in near_x:
         relayout(False, dx)
     pltpu.make_async_copy(s2.at[0, y], r2.at[0], in_sem.at[5]).start()
-    for dx, dy in SPREAD:
-        send_pol(False, dx, dy)
 
     wait_for(tw.at[pl.ds(1, 15)], tw_r.at[0])
     tots[0] = jnp.sum(tw[...], axis=0)
@@ -224,11 +222,16 @@
     def contract(first, half):
         src = r1 if first else r2
         at = 0 if half == 0 else ROWS1
-        w0 = src[:, :BODY].reshape(16 * BODY, 256)
-        w1 = src[:, BODY : 2 * BODY].reshape(16 * BODY, 256)
-        lt = r1[:, 2 * BODY :].astype(F32)
-        lt = lt[:, :8] if first else lt[:, 8:]
-        lt = lt.reshape(128, 256).astype(BF16)
+        def columns(lo):
+            return jnp.concatenate(
+                [src[:, at : at + BODY].reshape(16 * BODY, 128) for at in (lo, lo + 2 * BODY)],
+                axis=1,
+            )
+
+        w0, w1 = columns(0), columns(BODY)
+        lt = src[:, 4 * BODY :].astype(F32)
+        lt = jnp.concatenate([lt[:, :8].reshape(128, 128), lt[:, 8:].reshape(128, 128)], axis=1)
+        lt = lt.astype(BF16)
 
         def lanes(lo, hi):
             return jnp.concatenate(
@@ -261,6 +264,8 @@
     d_copies, z_copies = [], []
     for g in (2, 3, 4, 5):
         wait_for(arrive[g], ph_r.at[g])
+    for dx, dy in SPREAD:
+        send_pol(False, dx, dy)
     wait_for(r1.at[pl.ds(1, 15)], pol_r.at[0])
     wait_for(r1.at[0], in_sem.at[4])
     @pl.when(zh == 0)
@@ -327,10 +332,10 @@
             vmem((8, CH), jnp.int32),
             vmem((2, 256, 128), BF16),
             vmem((CH, 8, 128), F32),
-            vmem((X, Y, ROWS1, 256), BF16),
-            vmem((X, Y, ROWS2, 256), BF16),
-            vmem((16, ROWS1, 256), BF16),
-            vmem((16, ROWS2, 256), BF16),
+            vmem((X, Y, POL_ROWS, 128), BF16),
+            vmem((X, Y, POL_ROWS, 128), BF16),
+            vmem((16, POL_ROWS, 128), BF16),
+            vmem((16, POL_ROWS, 128), BF16),
             vmem((2, X, Y, PH_ROWS, 128), BF16),
             vmem((16, 1, 128), F32),
             vmem((8, 256, 256), F32),

time: 35.9 us -> 35.2 us (0.981)
  Pallas kernels: 35 us -> 34.3 us
    pallas_call x1, Pallas kernels: 35 us -> 34.3 us  [body(): pl.pallas_call(kernel, out_shape=jax.ShapeDtypeStruct((128, 2, 512), BF16...]
where the time goes in v4:
time: 35.2 us; the launch traced here: 35 us
  Pallas kernels  34.3 us (97%)
  local copies, waits for them, and re-layouts  0.71 us (2%)
    pallas_call x1, Pallas kernels, body(): pl.pallas_call(kernel, out_shape=jax.ShapeDtypeStruct((128, 2, 512), BF16...  34.3 us
    unnamed x1, local copies, waits for them, and re-layouts  0.71 us

profile of v4, /device:TPU:1, one launch (start us, length us, event | category | flops | bytes accessed | tf_op | source)
XLA Modules:
  0.0 35.0 jit_solution(5453649677327757135)
XLA Ops:
  0.0 34.3 %exchange.1 = bf16[128,2,512]{2,1,0:T(2,128)(2,1)S(1)} custom-call(bf16[2,36,8,1024]{3,2,1,0:T(8,128)(2,1)} %pol_hbm.1, bf16[36,2,512]{2,1,0:T(2,128)(2,1)} %bitcast.5, f32[1,36]{1,0:T(1,128)} %bitcast.7, s32[8,36]{1,0:T(8,128)} %bitcast.6), custom_call_target="tpu_custom_call" | custom-call | flops 1207959552 | bytes 2097152 | tf_op jit(solution)/shard_map/exchange/pallas_call | solution.py:323
  34.3 0.7 %copy.6 = bf16[1,16,8,2,512]{4,3,2,1,0:T(2,128)(2,1)} copy(bf16[1,16,8,2,512]{4,3,2,1,0:T(2,128)(2,1)S(1)} %bitcast.4) | data formatting | bytes 524288

commit v5 on v4

--- a/solution.py
+++ b/solution.py
@@ -153,7 +153,7 @@
     def wait_for(view, sem):
         pltpu.make_async_copy(view, view, sem).wait()
 
-    ring = (1, 3, 2)
+    ring = (2, 1, 3)
     rest = pl.ds(1, 3)
     rows_a, rows_b = pl.ds(0, ROWS1), pl.ds(ROWS1, ROWS2)
     arrive = [
@@ -174,7 +174,7 @@
         rcopy(ph.at[1, 0, 0], ph.at[1, d, 0], ph_s.at[3], ph_r.at[3], plane(d, 0)).start()
 
     def send_pol(first, dx, dy):
-        q = 0 if first else 1
+        q = 0 if first else 1 + dx
         src, dst = (s1, r1) if first else (s2, r2)
         rcopy(
             src.at[dx, lax.rem(y + dy, Y)], dst.at[dx * 4 + dy],
@@ -219,32 +219,41 @@
     ct = rcopy(tots.at[0], tots.at[1], t_s.at[0], t_r.at[0], core_peer)
     ct.start()
 
-    def contract(first, half):
+    def contract(first, half, xs):
         src = r1 if first else r2
         at = 0 if half == 0 else ROWS1
+        def taken(ref, rows):
+            return jnp.concatenate(
+                [ref[4 * dx : 4 * dx + 4, rows].reshape(-1, 128) for dx in xs], axis=0
+            )
+
         def columns(lo):
             return jnp.concatenate(
-                [src[:, at : at + BODY].reshape(16 * BODY, 128) for at in (lo, lo + 2 * BODY)],
+                [taken(src, slice(c, c + BODY)) for c in (lo, lo + 2 * BODY)], axis=1
+            )
+
+        w0, w1 = columns(0), columns(BODY)
+        count = 4 * len(xs)
+        lt = taken(src, slice(4 * BODY, POL_ROWS)).astype(F32).reshape(count, 16, 128)
+        lt = jnp.concatenate([lt[:, :8].reshape(-1, 128), lt[:, 8:].reshape(-1, 128)], axis=1)
+        lt = lt.astype(BF16)
+
+        def lanes(lo, hi):
+            return jnp.concatenate(
+                [
+                    jnp.concatenate([ph[s, dx, :, lo:hi].reshape(-1, 128) for dx in xs], axis=0)
+                    for s in range(2)
+                ],
                 axis=1,
             )
 
-        w0, w1 = columns(0), columns(BODY)
-        lt = src[:, 4 * BODY :].astype(F32)
-        lt = jnp.concatenate([lt[:, :8].reshape(128, 128), lt[:, 8:].reshape(128, 128)], axis=1)
-        lt = lt.astype(BF16)
-
-        def lanes(lo, hi):
-            return jnp.concatenate(
-                [ph[s, :, :, lo:hi].reshape(-1, 128) for s in range(2)], axis=1
-            )
-
         pr = lanes(at, at + BODY)
         pi = lanes(at + BODY, at + 2 * BODY)
-        pt = lanes(2 * BODY, ROWS1).reshape(16, 16, 256).astype(F32)
+        pt = lanes(2 * BODY, ROWS1).reshape(count, 16, 256).astype(F32)
         pt = pt[:, :8] if half == 0 else pt[:, 8:]
         turned = jnp.concatenate([-pt[:, 4:], pt[:, :4]], axis=1)
-        pt = pt.reshape(128, 256).astype(BF16)
-        turned = turned.reshape(128, 256).astype(BF16)
+        pt = pt.reshape(-1, 256).astype(BF16)
+        turned = turned.reshape(-1, 256).astype(BF16)
         yield tdot(w0, pr) - tdot(w1, pi) + tdot(lt, pt)
         yield tdot(w0, pi) + tdot(w1, pr) + tdot(lt, turned)
 
@@ -253,9 +262,9 @@
 
     def spread(first, half):
         copies = []
-        for k, value in enumerate(contract(first, half)):
+        for k, value in enumerate(contract(first, half, range(X) if first else (0, 2))):
             n = (0 if first else 4) + half * 2 + k
-            part[n] = value
+            part[n] = value if first else part[n] + value
             c = rcopy(part.at[n, pl.ds(theirs, 128)], d2d.at[n], d_s.at[n], d_r.at[n], core_peer)
             c.start()
             copies.append(c)
@@ -289,7 +298,14 @@
             c.start()
             z_copies.append(c)
 
-    wait_for(r2.at[pl.ds(1, 15)], pol_r.at[1])
+    own_slots = [pl.ds(1, 3)] + [pl.ds(4 * dx, 4) for dx in range(1, X)]
+    for dx in (1, 3):
+        wait_for(r2.at[own_slots[dx]], pol_r.at[1 + dx])
+    for half in range(2):
+        for k, value in enumerate(contract(False, half, (1, 3))):
+            part[4 + half * 2 + k] = value
+    for dx in (0, 2):
+        wait_for(r2.at[own_slots[dx]], pol_r.at[1 + dx])
     wait_for(r2.at[0], in_sem.at[5])
     d_copies += spread(False, 0) + spread(False, 1)
     cz.wait_recv()
@@ -313,7 +329,8 @@
     for g in range(8):
         wait_for(arrive[g], ph_s.at[g])
     wait_for(r1.at[pl.ds(1, 15)], pol_s.at[0])
-    wait_for(r2.at[pl.ds(1, 15)], pol_s.at[1])
+    for dx in range(X):
+        wait_for(r2.at[own_slots[dx]], pol_s.at[1 + dx])
     wait_for(tw.at[pl.ds(1, 15)], tw_s.at[0])
 
 
@@ -344,7 +361,7 @@
             vmem((4, 128, 256), BF16),
             vmem((4, 1, 128), F32),
             dma((6,)),
-            dma((2,)), dma((2,)),
+            dma((5,)), dma((5,)),
             dma((8,)), dma((8,)),
             dma((1,)), dma((1,)),
             dma((8,)), dma((8,)),

time: 35.2 us -> 35 us (level)
  no operation moved by 1% of the time
where the time goes in v5:
time: 35 us; the launch traced here: 34.9 us
  Pallas kernels  34.2 us (98%)
  local copies, waits for them, and re-layouts  0.71 us (2%)
    pallas_call x1, Pallas kernels, body(): pl.pallas_call(kernel, out_shape=jax.ShapeDtypeStruct((128, 2, 512), BF16...  34.2 us
    unnamed x1, local copies, waits for them, and re-layouts  0.71 us

profile of v5, /device:TPU:1, one launch (start us, length us, event | category | flops | bytes accessed | tf_op | source)
XLA Modules:
  0.0 34.9 jit_solution(17910318624201011076)
XLA Ops:
  0.0 34.2 %exchange.1 = bf16[128,2,512]{2,1,0:T(2,128)(2,1)S(1)} custom-call(bf16[2,36,8,1024]{3,2,1,0:T(8,128)(2,1)} %pol_hbm.1, bf16[36,2,512]{2,1,0:T(2,128)(2,1)} %bitcast.5, f32[1,36]{1,0:T(1,128)} %bitcast.7, s32[8,36]{1,0:T(8,128)} %bitcast.6), custom_call_target="tpu_custom_call" | custom-call | flops 1207959552 | bytes 2097152 | tf_op jit(solution)/shard_map/exchange/pallas_call | solution.py:340
  34.2 0.7 %copy.6 = bf16[1,16,8,2,512]{4,3,2,1,0:T(2,128)(2,1)} copy(bf16[1,16,8,2,512]{4,3,2,1,0:T(2,128)(2,1)S(1)} %bitcast.4) | data formatting | bytes 524288

commit v6 on v5

--- a/solution.py
+++ b/solution.py
@@ -219,7 +219,7 @@
     ct = rcopy(tots.at[0], tots.at[1], t_s.at[0], t_r.at[0], core_peer)
     ct.start()
 
-    def contract(first, half, xs):
+    def contract(first, half, xs, cc):
         src = r1 if first else r2
         at = 0 if half == 0 else ROWS1
         def taken(ref, rows):
@@ -228,15 +228,12 @@
             )
 
         def columns(lo):
-            return jnp.concatenate(
-                [taken(src, slice(c, c + BODY)) for c in (lo, lo + 2 * BODY)], axis=1
-            )
+            return taken(src, pl.ds(pl.multiple_of(cc * 2 * BODY + lo, 16), BODY))
 
         w0, w1 = columns(0), columns(BODY)
         count = 4 * len(xs)
         lt = taken(src, slice(4 * BODY, POL_ROWS)).astype(F32).reshape(count, 16, 128)
-        lt = jnp.concatenate([lt[:, :8].reshape(-1, 128), lt[:, 8:].reshape(-1, 128)], axis=1)
-        lt = lt.astype(BF16)
+        lt = jnp.where(cc == 0, lt[:, :8], lt[:, 8:]).reshape(-1, 128).astype(BF16)
 
         def lanes(lo, hi):
             return jnp.concatenate(
@@ -260,14 +257,22 @@
     mine = pl.multiple_of(core * 128, 128)
     theirs = pl.multiple_of((1 - core) * 128, 128)
 
+    def sums(first, half, xs, cc, add):
+        rows = pl.ds(pl.multiple_of(cc * 128, 128), 128)
+        for k, value in enumerate(contract(first, half, xs, cc)):
+            n = (0 if first else 4) + half * 2 + k
+            part[n, rows] = part[n, rows] + value if add else value
+            yield n
+
     def spread(first, half):
+        xs = range(X) if first else (0, 2)
         copies = []
-        for k, value in enumerate(contract(first, half, range(X) if first else (0, 2))):
-            n = (0 if first else 4) + half * 2 + k
-            part[n] = value if first else part[n] + value
+        for n in sums(first, half, xs, 1 - core, not first):
             c = rcopy(part.at[n, pl.ds(theirs, 128)], d2d.at[n], d_s.at[n], d_r.at[n], core_peer)
             c.start()
             copies.append(c)
+        for _ in sums(first, half, xs, core, not first):
+            pass
         return copies
 
     d_copies, z_copies = [], []
@@ -302,8 +307,9 @@
     for dx in (1, 3):
         wait_for(r2.at[own_slots[dx]], pol_r.at[1 + dx])
     for half in range(2):
-        for k, value in enumerate(contract(False, half, (1, 3))):
-            part[4 + half * 2 + k] = value
+        for cc in (1 - core, core):
+            for _ in sums(False, half, (1, 3), cc, False):
+                pass
     for dx in (0, 2):
         wait_for(r2.at[own_slots[dx]], pol_r.at[1 + dx])
     wait_for(r2.at[0], in_sem.at[5])

time: 35 us -> 35 us (level)
  no operation moved by 1% of the time
where the time goes in v6:
time: 35 us; the launch traced here: 34.9 us
  Pallas kernels  34.2 us (98%)
  local copies, waits for them, and re-layouts  0.71 us (2%)
    pallas_call x1, Pallas kernels, body(): pl.pallas_call(kernel, out_shape=jax.ShapeDtypeStruct((128, 2, 512), BF16...  34.2 us
    unnamed x1, local copies, waits for them, and re-layouts  0.71 us

profile of v6, /device:TPU:1, one launch (start us, length us, event | category | flops | bytes accessed | tf_op | source)
XLA Modules:
  0.0 34.9 jit_solution(9375282167937541289)
XLA Ops:
  0.0 34.2 %exchange.1 = bf16[128,2,512]{2,1,0:T(2,128)(2,1)S(1)} custom-call(bf16[2,36,8,1024]{3,2,1,0:T(8,128)(2,1)} %pol_hbm.1, bf16[36,2,512]{2,1,0:T(2,128)(2,1)} %bitcast.5, f32[1,36]{1,0:T(1,128)} %bitcast.7, s32[8,36]{1,0:T(8,128)} %bitcast.6), custom_call_target="tpu_custom_call" | custom-call | flops 1207959552 | bytes 2097152 | tf_op jit(solution)/shard_map/exchange/pallas_call | solution.py:346
  34.2 0.7 %copy.6 = bf16[1,16,8,2,512]{4,3,2,1,0:T(2,128)(2,1)} copy(bf16[1,16,8,2,512]{4,3,2,1,0:T(2,128)(2,1)S(1)} %bitcast.4) | data formatting | bytes 524288

commit v7 on v6

--- a/solution.py
+++ b/solution.py
@@ -11,6 +11,7 @@
 
 X, Y = 4, 4
 SPREAD = [(dx, dy) for dx in (1, 3, 0, 2) for dy in range(Y) if dx or dy]
+FAR = sorted(SPREAD, key=lambda o: -(0, 1, 2, 1)[o[0]] - (0, 1, 2, 1)[o[1]])
 CH = 36
 BODY = 32
 ROWS1 = 2 * BODY + 16
@@ -186,7 +187,7 @@
         k = dx * 4 + dy
         rcopy(tw.at[0], tw.at[k], tw_s.at[0], tw_r.at[0], plane(dx, dy)).start()
 
-    for dx, dy in SPREAD:
+    for dx, dy in FAR:
         send_pol(True, dx, dy)
 
     def forward(q, strip, rows):

time: 35 us -> 35 us (level)
  no operation moved by 1% of the time
where the time goes in v7:
time: 35 us; the launch traced here: 34.9 us
  Pallas kernels  34.2 us (98%)
  local copies, waits for them, and re-layouts  0.71 us (2%)
    pallas_call x1, Pallas kernels, body(): pl.pallas_call(kernel, out_shape=jax.ShapeDtypeStruct((128, 2, 512), BF16...  34.2 us
    unnamed x1, local copies, waits for them, and re-layouts  0.71 us

profile of v7, /device:TPU:1, one launch (start us, length us, event | category | flops | bytes accessed | tf_op | source)
XLA Modules:
  0.0 34.9 jit_solution(8027938140443373111)
XLA Ops:
  0.0 34.2 %exchange.1 = bf16[128,2,512]{2,1,0:T(2,128)(2,1)S(1)} custom-call(bf16[2,36,8,1024]{3,2,1,0:T(8,128)(2,1)} %pol_hbm.1, bf16[36,2,512]{2,1,0:T(2,128)(2,1)} %bitcast.5, f32[1,36]{1,0:T(1,128)} %bitcast.7, s32[8,36]{1,0:T(8,128)} %bitcast.6), custom_call_target="tpu_custom_call" | custom-call | flops 1207959552 | bytes 2097152 | tf_op jit(solution)/shard_map/exchange/pallas_call | solution.py:347
  34.2 0.7 %copy.6 = bf16[1,16,8,2,512]{4,3,2,1,0:T(2,128)(2,1)} copy(bf16[1,16,8,2,512]{4,3,2,1,0:T(2,128)(2,1)S(1)} %bitcast.4) | data formatting | bytes 524288
